TPU v7x, 32 devices: a whole 2x2x4 slice. The times are simulated.
32 devices in a mesh: grp: 8 (over z, x), rep: 4 (over y, core).
Axes of the slice: x: 2, y: 2, z: 4, core: 2. Of those that a mesh axis runs over, the one named last changes fastest.
Arguments:
- series: bfloat16 [256, 5632], P('grp'), may hold values from -6 to 6
- regressors: float32 [256, 24], P('grp'), may hold values from -3 to 3
- span_ids: int32 [256], replicated, may hold values from 0 to 3, never falling along the last dimension, each value on 1 to 128 neighbouring positions
- nuisance_count: int32 [1], replicated, may hold values from 12 to 24
- owner_order: int32 [8], replicated, may hold values from 0 to 7
- vectors: bfloat16 [5632, 64], P('grp'), may hold values from -0.3125 to 0.3125
Outputs:
- projected: float32 [5632, 64], P(('grp', 'rep'))
Inputs may be any that keep to these rules, and one draw needn't show every extreme that they name: `span_ids`: never falls along frames; each of the 4 spans holds 1 to 128 frames, one exactly 128. `owner_order`: blocks may name the same slab.
All inputs are finite; a program needn't handle non-finite values.
Results may differ from a plain program's by a relative error of at most 0.0095.
Values may be sent and summed in bfloat16 or wider, within the bound.
A program may use at most 64 MiB of HBM per device.

v0:
```python
import math
import jax
import jax.numpy as jnp
from jax import lax
from jax.sharding import PartitionSpec as P

BLOCKS = 8
fast_pole = 0.64
slow_pole = 0.955
corr_limit = 0.99
norm_eps = 1e-06


def spread_2(value, axis, root):
    mine = lax.axis_index(axis) == root
    return lax.psum(jnp.where(mine, value, jnp.zeros_like(value)), axis)


def fisher_map(correlation):
    clipped = jnp.clip(correlation, -corr_limit, corr_limit)
    return 0.5 * jnp.log((1.0 + clipped) / (1.0 - clipped))


def block_operators(span_ids, frames):
    offsets = jnp.arange(128)
    lag_steps = offsets[:, None] - offsets[None, :]
    lag_clip = jnp.maximum(lag_steps, 0).astype(jnp.float32)
    operators = []
    for number in range(frames // 128):
        ids_here = span_ids[number * 128 : (number + 1) * 128]
        joined = (ids_here[:, None] == ids_here[None, :]) & (lag_steps >= 0)
        if number == 0:
            linked = jnp.zeros((128,), jnp.float32)
        else:
            linked = (ids_here == span_ids[number * 128 - 1]).astype(jnp.float32)
        pole_pair = []
        for pole_value in (fast_pole, slow_pole):
            matrix = jnp.where(
                joined, (1.0 - pole_value) * jnp.exp(lag_clip * math.log(pole_value)), 0.0
            )
            carried = linked * jnp.exp((offsets + 1).astype(jnp.float32) * math.log(pole_value))
            pole_pair.append((matrix, carried))
        operators.append(pole_pair)
    return operators


def band_pass(columns_in, operators):
    col_count = columns_in.shape[1]
    states = [jnp.zeros((col_count,), jnp.float32), jnp.zeros((col_count,), jnp.float32)]
    pieces = []
    for number, pole_pair in enumerate(operators):
        segment = columns_in[number * 128 : (number + 1) * 128]
        outputs = []
        for pole_slot in range(2):
            matrix, carried = pole_pair[pole_slot]
            response = (
                jnp.dot(matrix, segment, precision=lax.Precision.HIGHEST)
                + carried[:, None] * states[pole_slot][None, :]
            )
            states[pole_slot] = response[-1]
            outputs.append(response)
        pieces.append(outputs[0] - outputs[1])
    return jnp.concatenate(pieces, axis=0)


def nuisance_basis(filtered_nuisance, nuisance_count):
    active = (jnp.arange(filtered_nuisance.shape[1]) < nuisance_count[0]).astype(jnp.float32)
    masked = filtered_nuisance * active[None, :]
    gram_matrix = jnp.dot(masked.T, masked, precision=lax.Precision.HIGHEST) + jnp.diag(
        1.0 - active
    )
    return (masked, jnp.linalg.cholesky(gram_matrix))


def scale_columns(filtered, masked, lower_factor):
    highest = lax.Precision.HIGHEST
    right_side = jnp.dot(masked.T, filtered, precision=highest)
    halfway = lax.linalg.triangular_solve(lower_factor, right_side, left_side=True, lower=True)
    coefficients = lax.linalg.triangular_solve(
        lower_factor, halfway, left_side=True, lower=True, transpose_a=True
    )
    cleaned = filtered - jnp.dot(masked, coefficients, precision=highest)
    centered = cleaned - jnp.mean(cleaned, axis=0, keepdims=True)
    spread = lax.rsqrt(jnp.mean(centered * centered, axis=0, keepdims=True) + norm_eps)
    return (centered * spread * (1.0 / math.sqrt(centered.shape[0]))).astype(jnp.bfloat16)


def fold_tile(my_cols, vec_slab, running, part_cols):
    correlation = lax.dot_general(
        my_cols, part_cols, (((0,), (0,)), ((), ())), preferred_element_type=jnp.float32
    )
    fisher = fisher_map(correlation).astype(jnp.bfloat16)
    return running + jnp.dot(fisher, vec_slab, preferred_element_type=jnp.float32)


def local(series, regressors, span_ids, nuisance_count, owner_order, vectors):
    grp_count = lax.axis_size("grp")
    rep_count = lax.axis_size("rep")
    rep_index = lax.axis_index("rep")
    frames_loc = series.shape[0]
    frames = frames_loc * grp_count
    own_cols = series.shape[1] // (grp_count * rep_count)
    operators = block_operators(span_ids, frames)
    nuisance = lax.all_gather(regressors, "grp", axis=0, tiled=True)
    masked, lower_factor = nuisance_basis(band_pass(nuisance, operators), nuisance_count)
    quarter = series.reshape(frames_loc, grp_count, rep_count, own_cols)
    quarter = lax.dynamic_slice_in_dim(quarter, rep_index, 1, 2).reshape(
        frames_loc, grp_count, own_cols
    )
    filtered = band_pass(
        lax.all_to_all(quarter, "grp", split_axis=1, concat_axis=0, tiled=True)[:, 0, :].astype(
            jnp.float32
        ),
        operators,
    )
    unit_cols = scale_columns(filtered, masked, lower_factor)
    projected = jnp.zeros((own_cols, vectors.shape[1]), jnp.float32)
    for number in range(BLOCKS):
        piece_in, vec_slab = (
            spread_2(unit_cols, "grp", owner_order[number]),
            spread_2(vectors, "grp", owner_order[number]),
        )
        projected = fold_tile(
            unit_cols, vec_slab, projected, lax.all_gather(piece_in, "rep", axis=1, tiled=True)
        )
    return projected


def solution(mesh):
    placed = (P("grp", None), P("grp", None), P(), P(), P(), P("grp", None))
    return jax.shard_map(
        local, mesh=mesh, in_specs=placed, out_specs=P(("grp", "rep"), None), check_vma=False
    )
```

profile of v0, /device:TPU:0, one launch (start us, length us, event | category | flops | bytes accessed | tf_op | source)
XLA Modules:
  0.0 231.1 jit_solution(4362847719951692597)
XLA Ops:
  6.5 2.0 reshape.62
  8.5 0.3 constant_dynamic-slice_fusion
  8.8 0.7 copy.24
  9.6 7.3 %all-to-all-start = ((bf16[32,8,176]{2,0,1:T(8,128)(2,1)}), bf16[32,8,176]{2,0,1:T(8,128)(2,1)S(1)}, u32[]{:S(2)}, u32[]{:S(2)}) async-start(bf16[32,8,176]{2,0,1:T(8,128)(2,1)} %bitcast.70), calls=%async_computation | async-start | bytes 262144 | tf_op jit(solution)/shard_map/all_to_all | solution.py:111
  16.9 0.7 copy-done.10
  17.5 0.6 slice.91
  18.8 0.7 compare_select_fusion
  19.5 0.7 fusion.173
  25.2 31.1 %all-gather = f32[8,32,24]{1,2,0:T(8,128)S(1)} all-gather(f32[1,32,24]{1,2,0:T(8,128)S(1)} %bitcast.78), channel_id=1, replica_groups=mesh['grp'=8,'rep'=4] {'grp'}, dimensions={0}, use_global_device_ids=true | all-gather | bytes 27648 | tf_op jit(solution)/shard_map/all_gather | solution.py:104
  56.9 0.3 fusion.175
  57.7 0.3 fusion.1
  58.4 2.2 cholesky.16
  60.7 0.6 compare_reduce_fusion
  61.3 0.6 fusion.93
  62.0 1.9 custom-call.8
  63.8 0.9 broadcast_select_fusion
  64.8 0.3 convolution_add_fusion.2
  65.2 0.3 fusion.174
  65.7 0.3 convolution_add_fusion.1
  66.0 0.3 fusion
  66.3 0.3 fusion.35
  67.0 0.5 fusion.176
  67.6 0.8 broadcast_select_fusion.8
  68.4 0.9 broadcast_select_fusion.9
  69.3 95.1 %all-reduce.3.cloned.1.call-done = (bf16[704,64]{0,1:T(8,128)(2,1)}, bf16[256,176]{0,1:T(8,128)(2,1)}, bf16[704,64]{0,1:T(8,128)(2,1)}, bf16[256,176]{0,1:T(8,12...) async-done(((bf16[704,64]{0,1:T(8,128)(2,1)}, ...) | async-done | bytes 1441808 | tf_op jit(solution)/shard_map/psum | solution.py:16
  164.5 6.7 %all_gather.28 = bf16[256,704]{0,1:T(8,128)(2,1)S(1)} all-gather(bf16[256,176]{0,1:T(8,128)(2,1)} %get-tuple-element.6), channel_id=1, replica_groups=mesh['grp'=8,'rep'=4] {'rep'}, dimensions={1}, use_global_device_ids=true | all-gather | bytes 450560 | tf_op jit(solution)/shard_map/all_gather | solution.py:124
  171.2 6.5 %all_gather.29 = bf16[256,704]{0,1:T(8,128)(2,1)S(1)} all-gather(bf16[256,176]{0,1:T(8,128)(2,1)S(1)} %copy-done.7), channel_id=1, replica_groups=mesh['grp'=8,'rep'=4] {'rep'}, dimensions={1}, use_global_device_ids=true | all-gather | bytes 450560 | tf_op jit(solution)/shard_map/all_gather | solution.py:124
  177.7 6.5 %all_gather.30 = bf16[256,704]{0,1:T(8,128)(2,1)S(1)} all-gather(bf16[256,176]{0,1:T(8,128)(2,1)S(1)} %copy-done.6), channel_id=1, replica_groups=mesh['grp'=8,'rep'=4] {'rep'}, dimensions={1}, use_global_device_ids=true | all-gather | bytes 450560 | tf_op jit(solution)/shard_map/all_gather | solution.py:124
  184.2 6.5 %all_gather.31 = bf16[256,704]{0,1:T(8,128)(2,1)S(1)} all-gather(bf16[256,176]{0,1:T(8,128)(2,1)S(1)} %copy-done.5), channel_id=1, replica_groups=mesh['grp'=8,'rep'=4] {'rep'}, dimensions={1}, use_global_device_ids=true | all-gather | bytes 450560 | tf_op jit(solution)/shard_map/all_gather | solution.py:124
  190.7 6.5 %all_gather.32 = bf16[256,704]{0,1:T(8,128)(2,1)S(1)} all-gather(bf16[256,176]{0,1:T(8,128)(2,1)S(1)} %copy-done.4), channel_id=1, replica_groups=mesh['grp'=8,'rep'=4] {'rep'}, dimensions={1}, use_global_device_ids=true | all-gather | bytes 450560 | tf_op jit(solution)/shard_map/all_gather | solution.py:124
  197.3 6.5 %all_gather.33 = bf16[256,704]{0,1:T(8,128)(2,1)S(1)} all-gather(bf16[256,176]{0,1:T(8,128)(2,1)S(1)} %copy-done.3), channel_id=1, replica_groups=mesh['grp'=8,'rep'=4] {'rep'}, dimensions={1}, use_global_device_ids=true | all-gather | bytes 450560 | tf_op jit(solution)/shard_map/all_gather | solution.py:124
  203.8 6.5 %all_gather.34 = bf16[256,704]{0,1:T(8,128)(2,1)S(1)} all-gather(bf16[256,176]{0,1:T(8,128)(2,1)S(1)} %copy-done.2), channel_id=1, replica_groups=mesh['grp'=8,'rep'=4] {'rep'}, dimensions={1}, use_global_device_ids=true | all-gather | bytes 450560 | tf_op jit(solution)/shard_map/all_gather | solution.py:124
  210.3 6.5 %all_gather.35 = bf16[256,704]{0,1:T(8,128)(2,1)S(1)} all-gather(bf16[256,176]{0,1:T(8,128)(2,1)S(1)} %copy-done.1), channel_id=1, replica_groups=mesh['grp'=8,'rep'=4] {'rep'}, dimensions={1}, use_global_device_ids=true | all-gather | bytes 450560 | tf_op jit(solution)/shard_map/all_gather | solution.py:124
  216.8 0.5 fusion.2
  217.3 0.4 copy-done.17
  217.7 0.5 convolution_add_fusion.10
  218.2 0.4 copy-done.16
  218.6 0.5 convolution_add_fusion.9
  219.1 0.4 copy-done.15
  219.5 0.5 convolution_add_fusion.8
  220.0 0.4 copy-done.14
  220.4 0.5 convolution_add_fusion.7
  220.9 0.4 copy-done.13
  221.3 0.5 convolution_add_fusion.6
  221.8 0.4 copy-done.12
  222.2 0.5 convolution_add_fusion.5
  222.7 0.4 copy-done.11
  223.1 1.1 convolution_add_fusion.4
  (59 shorter events, 2.6 us)
Async XLA Ops:
  9.6 55.2 %all-to-all-start = ((bf16[32,8,176]{2,0,1:T(8,128)(2,1)}), bf16[32,8,176]{2,0,1:T(8,128)(2,1)S(1)}, u32[]{:S(2)}, u32[]{:S(2)}) async-start(bf16[32,8,176]{2,0,1:T(8,128)(2,1)} %bitcast.70), calls=%async_computation | async-start | bytes 262144 | tf_op jit(solution)/shard_map/all_to_all | solution.py:111
  16.8 147.6 %all-reduce.3.cloned.1.call-start = ((), (), s32[]{:S(2)}) async-start(), calls=%async_computation.1 | async-start | bytes 3014656 | tf_op jit(solution)/shard_map/psum | solution.py:16
  16.9 0.7 copy-start.10
  18.8 0.7 copy-start.8
  22.6 2.6 %copy-start.9 = (f32[32,24]{0,1:T(8,128)S(1)}, f32[32,24]{0,1:T(8,128)}, u32[]{:S(2)}) copy-start(f32[32,24]{0,1:T(8,128)} %param.7) | copy-start | bytes 9220
  58.1 5.8 %copy-start = (bf16[704,64]{0,1:T(8,128)(2,1)S(1)}, bf16[704,64]{0,1:T(8,128)(2,1)}, u32[]{:S(2)}) copy-start(bf16[704,64]{0,1:T(8,128)(2,1)} %param.11) | copy-start | bytes 270340
  164.5 6.7 %copy-start.7 = (bf16[256,176]{0,1:T(8,128)(2,1)S(1)}, bf16[256,176]{0,1:T(8,128)(2,1)}, u32[]{:S(2)}) copy-start(bf16[256,176]{0,1:T(8,128)(2,1)} %get-tuple-element.8) | copy-start | bytes 270340
  171.2 6.5 %copy-start.6 = (bf16[256,176]{0,1:T(8,128)(2,1)S(1)}, bf16[256,176]{0,1:T(8,128)(2,1)}, u32[]{:S(2)}) copy-start(bf16[256,176]{0,1:T(8,128)(2,1)} %get-tuple-element.10) | copy-start | bytes 270340
  177.7 6.5 %copy-start.5 = (bf16[256,176]{0,1:T(8,128)(2,1)S(1)}, bf16[256,176]{0,1:T(8,128)(2,1)}, u32[]{:S(2)}) copy-start(bf16[256,176]{0,1:T(8,128)(2,1)} %get-tuple-element.12) | copy-start | bytes 270340
  184.2 6.5 %copy-start.4 = (bf16[256,176]{0,1:T(8,128)(2,1)S(1)}, bf16[256,176]{0,1:T(8,128)(2,1)}, u32[]{:S(2)}) copy-start(bf16[256,176]{0,1:T(8,128)(2,1)} %get-tuple-element.14) | copy-start | bytes 270340
  190.7 6.5 %copy-start.3 = (bf16[256,176]{0,1:T(8,128)(2,1)S(1)}, bf16[256,176]{0,1:T(8,128)(2,1)}, u32[]{:S(2)}) copy-start(bf16[256,176]{0,1:T(8,128)(2,1)} %get-tuple-element.16) | copy-start | bytes 270340
  197.3 6.5 %copy-start.2 = (bf16[256,176]{0,1:T(8,128)(2,1)S(1)}, bf16[256,176]{0,1:T(8,128)(2,1)}, u32[]{:S(2)}) copy-start(bf16[256,176]{0,1:T(8,128)(2,1)} %get-tuple-element.18) | copy-start | bytes 270340
  203.8 6.5 %copy-start.1 = (bf16[256,176]{0,1:T(8,128)(2,1)S(1)}, bf16[256,176]{0,1:T(8,128)(2,1)}, u32[]{:S(2)}) copy-start(bf16[256,176]{0,1:T(8,128)(2,1)} %get-tuple-element.20) | copy-start | bytes 270340
  210.3 6.5 %copy-start.18 = (bf16[704,64]{0,1:T(8,128)(2,1)S(1)}, bf16[704,64]{0,1:T(8,128)(2,1)}, u32[]{:S(2)}) copy-start(bf16[704,64]{0,1:T(8,128)(2,1)} %get-tuple-element.5) | copy-start | bytes 270340
  216.8 0.9 copy-start.17
  217.7 0.9 copy-start.16
  218.6 0.9 copy-start.15
  219.5 0.9 copy-start.14
  220.4 0.9 copy-start.13
  221.3 0.9 copy-start.12
  222.2 0.9 copy-start.11
Sparse Core Ops, SparseCore 0:
  69.4 94.9 all-reduce.2
where the time goes:
time: 232 us; the launch traced here: 231 us
  waiting for transfers between devices  95.1 us (41%)
  blocking collectives  83.4 us (36%)
  between operations  19.4 us (8%)
  other arithmetic  8.9 us (4%)
  local copies, waits for them, and re-layouts  8.67 us (4%)
  matrix products  8.23 us (4%)
  starting transfers between devices  7.29 us (3%)
    psum x1, waiting for transfers between devices, spread_2(): return lax.psum(jnp.where(mine, value, jnp.zeros_like(value)), axis)  95.1 us
    all_gather x8, blocking collectives, local(): lax.all_gather(piece_in, 'rep', axis=1, tiled=True)  52.3 us
    all_gather x1, blocking collectives, local(): nuisance = lax.all_gather(regressors, 'grp', axis=0, tiled=True)  31.1 us
    all_to_all x1, starting transfers between devices, local(): lax.all_to_all(quarter, 'grp', split_axis=1, concat_axis=0, tiled=True)  7.25 us
    dot_general x8, matrix products, fold_tile(): jnp.dot(fisher, vec_slab, preferred_element_type=jnp.float32)  4.66 us
  transfers between devices with their start and end apart: 2, of which 1 were waited for; matrix products, arithmetic and copies ran while one was open for 4% of the time, Pallas kernels for 0%

commit v1 on v0

--- a/solution.py
+++ b/solution.py
@@ -9,6 +9,18 @@
 slow_pole = 0.955
 corr_limit = 0.99
 norm_eps = 1e-06
+
+
+def change_edges(mat, link_axis):
+    return jnp.concatenate(
+        lax.all_to_all(
+            jnp.stack(jnp.split(mat, lax.psum(1, axis_name=link_axis), 1), 0),
+            axis_name=link_axis,
+            split_axis=0,
+            concat_axis=0,
+        ),
+        0,
+    )
 
 
 def spread_2(value, axis, root):
@@ -107,12 +119,7 @@
     quarter = lax.dynamic_slice_in_dim(quarter, rep_index, 1, 2).reshape(
         frames_loc, grp_count, own_cols
     )
-    filtered = band_pass(
-        lax.all_to_all(quarter, "grp", split_axis=1, concat_axis=0, tiled=True)[:, 0, :].astype(
-            jnp.float32
-        ),
-        operators,
-    )
+    filtered = band_pass(change_edges(quarter, "grp")[:, 0, :].astype(jnp.float32), operators)
     unit_cols = scale_columns(filtered, masked, lower_factor)
     projected = jnp.zeros((own_cols, vectors.shape[1]), jnp.float32)
     for number in range(BLOCKS):

time: 232 us -> 236 us (1.017)
  local copies, waits for them, and re-layouts: 8.67 us -> 13 us
    unnamed x38 -> x46, local copies, waits for them, and re-layouts: 3.38 us -> 7.62 us
where the time goes in v1:
time: 236 us
  waiting for transfers between devices  95.1 us (40%)
  blocking collectives  83.4 us (35%)
  between operations  19.5 us (8%)
  local copies, waits for them, and re-layouts  13 us (6%)
  other arithmetic  8.86 us (4%)
  matrix products  8.23 us (3%)
  starting transfers between devices  7.29 us (3%)
    psum x1, waiting for transfers between devices, spread_2(): return lax.psum(jnp.where(mine, value, jnp.zeros_like(value)), axis)  95.1 us
    all_gather x8, blocking collectives, local(): lax.all_gather(piece_in, 'rep', axis=1, tiled=True)  52.3 us
    all_gather x1, blocking collectives, local(): nuisance = lax.all_gather(regressors, 'grp', axis=0, tiled=True)  31.1 us
    unnamed x46, local copies, waits for them, and re-layouts  7.62 us
    all_to_all x1, starting transfers between devices, change_edges(): lax.all_to_all(jnp.stack(jnp.split(mat, lax.psum(1, axis_name=link_axis),...  7.25 us
  transfers between devices with their start and end apart: 2, of which 1 were waited for; matrix products, arithmetic and copies ran while one was open for 4% of the time, Pallas kernels for 0%

profile of v1, /device:TPU:0, one launch (start us, length us, event | category | flops | bytes accessed | tf_op | source)
XLA Modules:
  0.0 235.5 jit_solution(630950272272020619)
XLA Ops:
  6.5 2.0 reshape.61
  9.1 0.6 constant_dynamic-update-slice_fusion.7
  9.7 0.6 constant_dynamic-update-slice_fusion.6
  10.3 0.6 constant_dynamic-update-slice_fusion.5
  10.9 0.6 constant_dynamic-update-slice_fusion.4
  11.5 0.6 constant_dynamic-update-slice_fusion.3
  12.1 0.6 constant_dynamic-update-slice_fusion.2
  12.7 0.6 constant_dynamic-update-slice_fusion.1
  13.3 0.6 constant_dynamic-update-slice_fusion
  13.9 7.3 %all-to-all-start = ((bf16[8,32,1,176]{3,1,2,0:T(8,128)(2,1)}), bf16[8,32,1,176]{3,1,2,0:T(8,128)(2,1)S(1)}, u32[]{:S(2)}, u32[]{:S(2)}) async-start(bf16[8,32,1,176]{3,1,2,0:T(8,128)(2,1)} %constant_dynamic-update-slice_fusion), calls=%async_computation | async-start | bytes 262144 | tf_op jit(solution)/shard_map/all_to_all | solution.py:16
  21.3 0.7 copy-done.10
  21.9 0.6 slice.91
  23.2 0.7 compare_select_fusion
  23.9 0.7 fusion.174
  29.7 31.1 %all-gather = f32[8,32,24]{1,2,0:T(8,128)S(1)} all-gather(f32[1,32,24]{1,2,0:T(8,128)S(1)} %bitcast.91), channel_id=1, replica_groups=mesh['grp'=8,'rep'=4] {'grp'}, dimensions={0}, use_global_device_ids=true | all-gather | bytes 27648 | tf_op jit(solution)/shard_map/all_gather | solution.py:116
  62.9 2.2 cholesky.16
  65.2 0.6 compare_reduce_fusion
  65.8 0.6 fusion.93
  66.5 1.9 custom-call.8
  68.3 0.9 broadcast_select_fusion
  69.7 0.3 fusion.175
  71.4 0.5 fusion.177
  72.1 0.8 broadcast_select_fusion.8
  72.9 0.9 broadcast_select_fusion.9
  73.8 95.1 %all-reduce.3.cloned.1.call-done = (bf16[704,64]{0,1:T(8,128)(2,1)}, bf16[256,176]{0,1:T(8,128)(2,1)}, bf16[704,64]{0,1:T(8,128)(2,1)}, bf16[256,176]{0,1:T(8,12...) async-done(((bf16[704,64]{0,1:T(8,128)(2,1)}, ...) | async-done | bytes 1441808 | tf_op jit(solution)/shard_map/psum | solution.py:28
  168.9 6.7 %all_gather.28 = bf16[256,704]{0,1:T(8,128)(2,1)S(1)} all-gather(bf16[256,176]{0,1:T(8,128)(2,1)} %get-tuple-element.6), channel_id=1, replica_groups=mesh['grp'=8,'rep'=4] {'rep'}, dimensions={1}, use_global_device_ids=true | all-gather | bytes 450560 | tf_op jit(solution)/shard_map/all_gather | solution.py:131
  175.6 6.5 %all_gather.29 = bf16[256,704]{0,1:T(8,128)(2,1)S(1)} all-gather(bf16[256,176]{0,1:T(8,128)(2,1)S(1)} %copy-done.7), channel_id=1, replica_groups=mesh['grp'=8,'rep'=4] {'rep'}, dimensions={1}, use_global_device_ids=true | all-gather | bytes 450560 | tf_op jit(solution)/shard_map/all_gather | solution.py:131
  182.1 6.5 %all_gather.30 = bf16[256,704]{0,1:T(8,128)(2,1)S(1)} all-gather(bf16[256,176]{0,1:T(8,128)(2,1)S(1)} %copy-done.6), channel_id=1, replica_groups=mesh['grp'=8,'rep'=4] {'rep'}, dimensions={1}, use_global_device_ids=true | all-gather | bytes 450560 | tf_op jit(solution)/shard_map/all_gather | solution.py:131
  188.7 6.5 %all_gather.31 = bf16[256,704]{0,1:T(8,128)(2,1)S(1)} all-gather(bf16[256,176]{0,1:T(8,128)(2,1)S(1)} %copy-done.5), channel_id=1, replica_groups=mesh['grp'=8,'rep'=4] {'rep'}, dimensions={1}, use_global_device_ids=true | all-gather | bytes 450560 | tf_op jit(solution)/shard_map/all_gather | solution.py:131
  195.2 6.5 %all_gather.32 = bf16[256,704]{0,1:T(8,128)(2,1)S(1)} all-gather(bf16[256,176]{0,1:T(8,128)(2,1)S(1)} %copy-done.4), channel_id=1, replica_groups=mesh['grp'=8,'rep'=4] {'rep'}, dimensions={1}, use_global_device_ids=true | all-gather | bytes 450560 | tf_op jit(solution)/shard_map/all_gather | solution.py:131
  201.7 6.5 %all_gather.33 = bf16[256,704]{0,1:T(8,128)(2,1)S(1)} all-gather(bf16[256,176]{0,1:T(8,128)(2,1)S(1)} %copy-done.3), channel_id=1, replica_groups=mesh['grp'=8,'rep'=4] {'rep'}, dimensions={1}, use_global_device_ids=true | all-gather | bytes 450560 | tf_op jit(solution)/shard_map/all_gather | solution.py:131
  208.2 6.5 %all_gather.34 = bf16[256,704]{0,1:T(8,128)(2,1)S(1)} all-gather(bf16[256,176]{0,1:T(8,128)(2,1)S(1)} %copy-done.2), channel_id=1, replica_groups=mesh['grp'=8,'rep'=4] {'rep'}, dimensions={1}, use_global_device_ids=true | all-gather | bytes 450560 | tf_op jit(solution)/shard_map/all_gather | solution.py:131
  214.7 6.5 %all_gather.35 = bf16[256,704]{0,1:T(8,128)(2,1)S(1)} all-gather(bf16[256,176]{0,1:T(8,128)(2,1)S(1)} %copy-done.1), channel_id=1, replica_groups=mesh['grp'=8,'rep'=4] {'rep'}, dimensions={1}, use_global_device_ids=true | all-gather | bytes 450560 | tf_op jit(solution)/shard_map/all_gather | solution.py:131
  221.3 0.5 fusion.2
  221.8 0.4 copy-done.17
  222.2 0.5 convolution_add_fusion.10
  222.7 0.4 copy-done.16
  223.1 0.5 convolution_add_fusion.9
  223.6 0.4 copy-done.15
  223.9 0.5 convolution_add_fusion.8
  224.5 0.4 copy-done.14
  224.8 0.5 convolution_add_fusion.7
  225.4 0.4 copy-done.13
  225.7 0.5 convolution_add_fusion.6
  226.2 0.4 copy-done.12
  226.6 0.5 convolution_add_fusion.5
  227.1 0.4 copy-done.11
  227.5 1.1 convolution_add_fusion.4
  (68 shorter events, 4.8 us)
Async XLA Ops:
  13.9 55.3 %all-to-all-start = ((bf16[8,32,1,176]{3,1,2,0:T(8,128)(2,1)}), bf16[8,32,1,176]{3,1,2,0:T(8,128)(2,1)S(1)}, u32[]{:S(2)}, u32[]{:S(2)}) async-start(bf16[8,32,1,176]{3,1,2,0:T(8,128)(2,1)} %constant_dynamic-update-slice_fusion), calls=%async_computation | async-start | bytes 262144 | tf_op jit(solution)/shard_map/all_to_all | solution.py:16
  21.2 147.7 %all-reduce.3.cloned.1.call-start = ((), (), s32[]{:S(2)}) async-start(), calls=%async_computation.1 | async-start | bytes 3014656 | tf_op jit(solution)/shard_map/psum | solution.py:28
  21.2 0.7 copy-start.10
  23.2 0.7 copy-start.8
  27.1 2.6 %copy-start.9 = (f32[32,24]{0,1:T(8,128)S(1)}, f32[32,24]{0,1:T(8,128)}, u32[]{:S(2)}) copy-start(f32[32,24]{0,1:T(8,128)} %param.7) | copy-start | bytes 9220
  62.5 5.8 %copy-start = (bf16[704,64]{0,1:T(8,128)(2,1)S(1)}, bf16[704,64]{0,1:T(8,128)(2,1)}, u32[]{:S(2)}) copy-start(bf16[704,64]{0,1:T(8,128)(2,1)} %param.11) | copy-start | bytes 270340
  168.9 6.7 %copy-start.7 = (bf16[256,176]{0,1:T(8,128)(2,1)S(1)}, bf16[256,176]{0,1:T(8,128)(2,1)}, u32[]{:S(2)}) copy-start(bf16[256,176]{0,1:T(8,128)(2,1)} %get-tuple-element.8) | copy-start | bytes 270340
  175.6 6.5 %copy-start.6 = (bf16[256,176]{0,1:T(8,128)(2,1)S(1)}, bf16[256,176]{0,1:T(8,128)(2,1)}, u32[]{:S(2)}) copy-start(bf16[256,176]{0,1:T(8,128)(2,1)} %get-tuple-element.10) | copy-start | bytes 270340
  182.1 6.5 %copy-start.5 = (bf16[256,176]{0,1:T(8,128)(2,1)S(1)}, bf16[256,176]{0,1:T(8,128)(2,1)}, u32[]{:S(2)}) copy-start(bf16[256,176]{0,1:T(8,128)(2,1)} %get-tuple-element.12) | copy-start | bytes 270340
  188.7 6.5 %copy-start.4 = (bf16[256,176]{0,1:T(8,128)(2,1)S(1)}, bf16[256,176]{0,1:T(8,128)(2,1)}, u32[]{:S(2)}) copy-start(bf16[256,176]{0,1:T(8,128)(2,1)} %get-tuple-element.14) | copy-start | bytes 270340
  195.2 6.5 %copy-start.3 = (bf16[256,176]{0,1:T(8,128)(2,1)S(1)}, bf16[256,176]{0,1:T(8,128)(2,1)}, u32[]{:S(2)}) copy-start(bf16[256,176]{0,1:T(8,128)(2,1)} %get-tuple-element.16) | copy-start | bytes 270340
  201.7 6.5 %copy-start.2 = (bf16[256,176]{0,1:T(8,128)(2,1)S(1)}, bf16[256,176]{0,1:T(8,128)(2,1)}, u32[]{:S(2)}) copy-start(bf16[256,176]{0,1:T(8,128)(2,1)} %get-tuple-element.18) | copy-start | bytes 270340
  208.2 6.5 %copy-start.1 = (bf16[256,176]{0,1:T(8,128)(2,1)S(1)}, bf16[256,176]{0,1:T(8,128)(2,1)}, u32[]{:S(2)}) copy-start(bf16[256,176]{0,1:T(8,128)(2,1)} %get-tuple-element.20) | copy-start | bytes 270340
  214.7 6.5 %copy-start.18 = (bf16[704,64]{0,1:T(8,128)(2,1)S(1)}, bf16[704,64]{0,1:T(8,128)(2,1)}, u32[]{:S(2)}) copy-start(bf16[704,64]{0,1:T(8,128)(2,1)} %get-tuple-element.5) | copy-start | bytes 270340
  221.3 0.9 copy-start.17
  222.2 0.9 copy-start.16
  223.1 0.9 copy-start.15
  223.9 0.9 copy-start.14
  224.8 0.9 copy-start.13
  225.7 0.9 copy-start.12
  226.6 0.9 copy-start.11
Sparse Core Ops, SparseCore 0:
  73.9 94.9 all-reduce.2
